TPU v7x, 32 devices: a whole 2x2x4 slice. The times are simulated.
32 devices in a mesh: gy: 4 (over y, x), gx: 8 (over z, core).
Axes of the slice: x: 2, y: 2, z: 4, core: 2. Of those that a mesh axis runs over, the one named last changes fastest.
Arguments:
- fields: bfloat16 [4, 16, 16384], P('gy', None, 'gx'), may hold values from -6 to 6
- leaf_inverse: bfloat16 [4, 64, 256, 256], P('gy', 'gx'), may hold values from -0.375 to 0.375
- coupling: bfloat16 [4, 64, 64, 256], P('gy', 'gx'), may hold values from -0.375 to 0.375
- skeleton_index: int32 [4, 64, 64], P('gy', 'gx'), may hold values from 0 to 255, as said below
- up_coef: float32 [4, 24, 4, 512], P('gy', 'gx'), may hold values from -0.5 to 0.5
- down_coef: float32 [4, 24, 4, 512], P('gy', 'gx'), may hold values from -0.5 to 0.5
- merge_own: bfloat16 [4, 24, 512, 512], P('gy', 'gx'), may hold values from -0.1875 to 0.1875
- merge_other: bfloat16 [4, 24, 512, 512], P('gy', 'gx'), may hold values from -0.1875 to 0.1875
- top_inverse: bfloat16 [4, 4096, 512], P('gy', 'gx'), may hold values from -0.1875 to 0.1875
- compress: bfloat16 [4, 256, 512], P('gy', 'gx'), may hold values from -0.25 to 0.25
- top_couple: bfloat16 [1024, 1024], P(None, ('gy', 'gx')), may hold values from -0.375 to 0.375
Outputs:
- solution: float32 [4, 16, 16384], P('gy', None, 'gx')
Inputs may be any that keep to these rules, and one draw needn't show every extreme that they name: `skeleton_index`: the 64 positions of one box are distinct.
All inputs are finite; a program needn't handle non-finite values.
Results may differ from a plain program's by a relative error of at most 0.015.
Values may be sent and summed in bfloat16 or wider, within the bound.
A program may use at most 64 MiB of HBM per device.

v0:
```python
import jax
import jax.numpy as jnp
from jax import lax
from jax.sharding import PartitionSpec as P


def extended(block, sides, width):
    for axis, dim in sides:
        count = lax.axis_size(axis)
        forward = [(i, i + 1) for i in range(count - 1)]
        backward = [(target, source) for source, target in forward]
        low = lax.ppermute(
            lax.slice_in_dim(block, block.shape[dim] - width, None, axis=dim), axis, forward
        )
        high = lax.ppermute(lax.slice_in_dim(block, 0, width, axis=dim), axis, backward)
        block = jnp.concatenate([low, block, high], axis=dim)
    return block


def partner_2(shard, axis, stride):
    return lax.ppermute(shard, axis, [(i, i ^ 1 << stride) for i in range(lax.axis_size(axis))])


def neighbour_mix(padded, coefs):
    total = coefs[0] * padded[0, 1] + coefs[1] * padded[2, 1]
    return total + coefs[2] * padded[1, 0] + coefs[3] * padded[1, 2]


def right_transpose(values, matrix):
    return lax.dot_general(
        values, matrix, (((1,), (1,)), ((), ())), preferred_element_type=jnp.float32
    )


def body(
    fields,
    leaf_inverse,
    coupling,
    skeleton_index,
    up_coef,
    down_coef,
    merge_own,
    merge_other,
    top_inverse,
    compress,
    top_couple,
):
    field_count = fields.shape[1]
    box_count = leaf_inverse.shape[1]
    box_size = leaf_inverse.shape[2]
    skel_size = coupling.shape[2]
    skel_total = box_count * skel_size
    level_count = merge_own.shape[1]
    blocks = fields[0].reshape(field_count, box_count, box_size)
    inverse = leaf_inverse[0]
    weights = coupling[0]
    index = skeleton_index[0]
    own = merge_own[0]
    other = merge_other[0]
    up_rates = up_coef[0]
    down_rates = down_coef[0]
    positions = lax.broadcasted_iota(jnp.int32, (box_count, skel_size, box_size), 2)
    selector = index[:, :, None] == positions
    select_half = selector.astype(jnp.bfloat16)
    select_full = selector.astype(jnp.float32)
    solved = jnp.einsum("fbq,bqr->fbr", blocks, inverse, preferred_element_type=jnp.float32).astype(
        jnp.bfloat16
    )
    picked = jnp.einsum("fbq,bkq->fbk", blocks, select_half, preferred_element_type=jnp.float32)
    state = picked - jnp.einsum("fbq,bkq->fbk", solved, weights, preferred_element_type=jnp.float32)
    state = state.reshape(field_count, skel_total)
    for level in range(level_count):
        padded = extended(state[None, None], (("gy", 0), ("gx", 1)), 1)
        mixed = state - neighbour_mix(padded, up_rates[level])
        rounded = mixed.astype(jnp.bfloat16)
        partner = partner_2(rounded, "gx", level)
        state = jnp.dot(rounded, own[level], preferred_element_type=jnp.float32)
        state = state + jnp.dot(partner, other[level], preferred_element_type=jnp.float32)
    top_state = state.astype(jnp.bfloat16)
    comp = compress[0]
    small = right_transpose(top_state, comp).astype(jnp.bfloat16)
    row_values = lax.all_gather(small, "gx", axis=1, tiled=True)
    coarse = jnp.dot(
        lax.all_gather(row_values, "gy", axis=1, tiled=True),
        top_couple,
        preferred_element_type=jnp.float32,
    )
    state = jnp.dot(top_state, top_inverse[0], preferred_element_type=jnp.float32)
    state = state + jnp.dot(coarse.astype(jnp.bfloat16), comp, preferred_element_type=jnp.float32)
    for level in reversed(range(level_count)):
        rounded = state.astype(jnp.bfloat16)
        sent = right_transpose(rounded, other[level])
        received = partner_2(sent.astype(jnp.bfloat16), "gx", level).astype(sent.dtype)
        mixed = right_transpose(rounded, own[level]) + received
        padded = extended(mixed[None, None].astype(jnp.bfloat16), (("gy", 0), ("gx", 1)), 1).astype(
            jnp.float32
        )
        state = mixed - neighbour_mix(padded, down_rates[level])
    skeleton = state.reshape(field_count, box_count, skel_size)
    back = jnp.einsum(
        "fbk,bkq->fbq", skeleton.astype(jnp.bfloat16), weights, preferred_element_type=jnp.float32
    ).astype(jnp.bfloat16)
    fixed = jnp.einsum("fbq,bqr->fbr", back, inverse, preferred_element_type=jnp.float32)
    placed = jnp.einsum("fbk,bkq->fbq", skeleton, select_full, precision=lax.Precision.HIGHEST)
    result = solved.astype(jnp.float32) - fixed + placed
    return result.reshape(1, field_count, box_count * box_size)


def solution(mesh):
    placed = (
        P("gy", None, "gx"),
        P("gy", "gx", None, None),
        P("gy", "gx", None, None),
        P("gy", "gx", None),
        P("gy", "gx", None, None),
        P("gy", "gx", None, None),
        P("gy", "gx", None, None),
        P("gy", "gx", None, None),
        P("gy", "gx", None),
        P("gy", "gx", None),
        P(None, ("gy", "gx")),
    )
    return jax.shard_map(
        body, mesh=mesh, in_specs=placed, out_specs=P("gy", None, "gx"), check_vma=False
    )
```

profile of v0, /device:TPU:1, one launch (start us, length us, event | category | flops | bytes accessed | tf_op | source)
XLA Modules:
  0.0 153.9 jit_solution(160735021089724741)
XLA Ops:
  0.0 0.9 copy.40
  1.5 1.2 convolution_bitcast_fusion.2
  3.1 3.9 %collective-permute-start = (f32[1,1,16,512]{3,2,1,0:T(8,128)S(1)}, f32[1,1,16,512]{3,2,1,0:T(8,128)S(1)}, u32[]{:S(2)}, u32[]{:S(2)}) collective-permute-start(f32[1,1,16,512]{3,2,1,0:T(8,128)S(1)} %broadcast_in_dim_reshape.3), channel_id=1, source_target_pairs={{0,8},{8,16},{16,24},{1,9},{9,17},{17,25},{2,10},{10,18},{18,26},{... | collective-permute-start | bytes 98312 | tf_op jit(solution)/shard_map/ppermute | solution.py:12
  7.1 1.3 collective-permute-start.1
  8.4 3.3 %collective-permute-done.1 = f32[1,1,16,512]{3,2,1,0:T(8,128)S(1)} collective-permute-done((f32[1,1,16,512]{3,2,1,0:T(8,128)S(1)}, f32[1,1,16,512]{3,2,1,0:T(8,128)S(1)}, u32[]{:S(2)}, u32[]{:S(2)}) %collective-permute-start.1) | collective-permute-done | bytes 32800 | tf_op jit(solution)/shard_map/ppermute | solution.py:15
  11.7 5.2 %collective-permute-start.2 = (f32[3,1,16,512]{3,2,1,0:T(8,128)S(1)}, f32[3,1,16,512]{3,2,1,0:T(8,128)S(1)}, u32[]{:S(2)}, u32[]{:S(2)}) collective-permute-start(f32[3,1,16,512]{3,2,1,0:T(8,128)S(1)} %constant_dynamic-update-slice_fusion), channel_id=1, source_target_pairs={{0,1},{1,2},{2,3},{3,4},{4,5},{5,6},{6,7},{8,9},{9,10},{10,11},{11... | collective-permute-start | bytes 294920 | tf_op jit(solution)/shard_map/ppermute | solution.py:12
  16.9 1.9 %collective-permute-start.3 = (f32[3,1,16,512]{3,2,1,0:T(8,128)S(1)}, f32[3,1,16,512]{3,2,1,0:T(8,128)S(1)}, u32[]{:S(2)}, u32[]{:S(2)}) collective-permute-start(f32[3,1,16,512]{3,2,1,0:T(8,128)S(1)} %constant_dynamic-update-slice_fusion), channel_id=1, source_target_pairs={{1,0},{2,1},{3,2},{4,3},{5,4},{6,5},{7,6},{9,8},{10,9},{11,10},{12... | collective-permute-start | bytes 294920 | tf_op jit(solution)/shard_map/ppermute | solution.py:15
  19.5 3.4 %collective-permute-done.3 = f32[3,1,16,512]{3,2,1,0:T(8,128)S(1)} collective-permute-done((f32[3,1,16,512]{3,2,1,0:T(8,128)S(1)}, f32[3,1,16,512]{3,2,1,0:T(8,128)S(1)}, u32[]{:S(2)}, u32[]{:S(2)}) %collective-permute-start.3) | collective-permute-done | bytes 98336 | tf_op jit(solution)/shard_map/ppermute | solution.py:15
  23.3 1.3 fusion.26
  24.9 4.2 %collective-permute-start.5 = (f32[1,1,16,512]{3,2,1,0:T(8,128)S(1)}, f32[1,1,16,512]{3,2,1,0:T(8,128)S(1)}, u32[]{:S(2)}, u32[]{:S(2)}) collective-permute-start(f32[1,1,16,512]{3,2,1,0:T(8,128)S(1)} %bitcast.308), channel_id=1, source_target_pairs={{0,8},{8,16},{16,24},{1,9},{9,17},{17,25},{2,10},{10,18},{18,26},{... | collective-permute-start | bytes 98312 | tf_op jit(solution)/shard_map/ppermute | solution.py:12
  29.0 1.3 collective-permute-start.6
  30.3 3.3 %collective-permute-done.6 = f32[1,1,16,512]{3,2,1,0:T(8,128)S(1)} collective-permute-done((f32[1,1,16,512]{3,2,1,0:T(8,128)S(1)}, f32[1,1,16,512]{3,2,1,0:T(8,128)S(1)}, u32[]{:S(2)}, u32[]{:S(2)}) %collective-permute-start.6) | collective-permute-done | bytes 32800 | tf_op jit(solution)/shard_map/ppermute | solution.py:15
  33.7 5.0 %collective-permute-start.7 = (f32[3,1,16,512]{3,2,1,0:T(8,128)S(1)}, f32[3,1,16,512]{3,2,1,0:T(8,128)S(1)}, u32[]{:S(2)}, u32[]{:S(2)}) collective-permute-start(f32[3,1,16,512]{3,2,1,0:T(8,128)S(1)} %pad_maximum_fusion), channel_id=1, source_target_pairs={{0,1},{1,2},{2,3},{3,4},{4,5},{5,6},{6,7},{8,9},{9,10},{10,11},{11... | collective-permute-start | bytes 294920 | tf_op jit(solution)/shard_map/ppermute | solution.py:12
  38.7 1.9 %collective-permute-start.8 = (f32[3,1,16,512]{3,2,1,0:T(8,128)S(1)}, f32[3,1,16,512]{3,2,1,0:T(8,128)S(1)}, u32[]{:S(2)}, u32[]{:S(2)}) collective-permute-start(f32[3,1,16,512]{3,2,1,0:T(8,128)S(1)} %pad_maximum_fusion), channel_id=1, source_target_pairs={{1,0},{2,1},{3,2},{4,3},{5,4},{6,5},{7,6},{9,8},{10,9},{11,10},{12... | collective-permute-start | bytes 294920 | tf_op jit(solution)/shard_map/ppermute | solution.py:15
  40.6 4.0 %collective-permute-done.8 = f32[3,1,16,512]{3,2,1,0:T(8,128)S(1)} collective-permute-done((f32[3,1,16,512]{3,2,1,0:T(8,128)S(1)}, f32[3,1,16,512]{3,2,1,0:T(8,128)S(1)}, u32[]{:S(2)}, u32[]{:S(2)}) %collective-permute-start.8) | collective-permute-done | bytes 98336 | tf_op jit(solution)/shard_map/ppermute | solution.py:15
  44.7 1.4 collective-permute-start.9
  46.2 1.1 collective-permute-done.9
  47.5 3.1 %collective-permute-start.10 = (f32[1,1,16,512]{3,2,1,0:T(8,128)S(1)}, f32[1,1,16,512]{3,2,1,0:T(8,128)S(1)}, u32[]{:S(2)}, u32[]{:S(2)}) collective-permute-start(f32[1,1,16,512]{3,2,1,0:T(8,128)S(1)} %bitcast.305), channel_id=1, source_target_pairs={{0,8},{8,16},{16,24},{1,9},{9,17},{17,25},{2,10},{10,18},{18,26},{... | collective-permute-start | bytes 98312 | tf_op jit(solution)/shard_map/ppermute | solution.py:12
  50.6 1.3 collective-permute-start.11
  51.9 3.8 %collective-permute-done.11 = f32[1,1,16,512]{3,2,1,0:T(8,128)S(1)} collective-permute-done((f32[1,1,16,512]{3,2,1,0:T(8,128)S(1)}, f32[1,1,16,512]{3,2,1,0:T(8,128)S(1)}, u32[]{:S(2)}, u32[]{:S(2)}) %collective-permute-start.11) | collective-permute-done | bytes 32800 | tf_op jit(solution)/shard_map/ppermute | solution.py:15
  55.8 3.9 %collective-permute-start.12 = (f32[3,1,16,512]{3,2,1,0:T(8,128)S(1)}, f32[3,1,16,512]{3,2,1,0:T(8,128)S(1)}, u32[]{:S(2)}, u32[]{:S(2)}) collective-permute-start(f32[3,1,16,512]{3,2,1,0:T(8,128)S(1)} %pad_maximum_fusion.1), channel_id=1, source_target_pairs={{0,1},{1,2},{2,3},{3,4},{4,5},{5,6},{6,7},{8,9},{9,10},{10,11},{11... | collective-permute-start | bytes 294920 | tf_op jit(solution)/shard_map/ppermute | solution.py:12
  59.7 1.9 %collective-permute-start.13 = (f32[3,1,16,512]{3,2,1,0:T(8,128)S(1)}, f32[3,1,16,512]{3,2,1,0:T(8,128)S(1)}, u32[]{:S(2)}, u32[]{:S(2)}) collective-permute-start(f32[3,1,16,512]{3,2,1,0:T(8,128)S(1)} %pad_maximum_fusion.1), channel_id=1, source_target_pairs={{1,0},{2,1},{3,2},{4,3},{5,4},{6,5},{7,6},{9,8},{10,9},{11,10},{12... | collective-permute-start | bytes 294920 | tf_op jit(solution)/shard_map/ppermute | solution.py:15
  61.6 4.0 %collective-permute-done.13 = f32[3,1,16,512]{3,2,1,0:T(8,128)S(1)} collective-permute-done((f32[3,1,16,512]{3,2,1,0:T(8,128)S(1)}, f32[3,1,16,512]{3,2,1,0:T(8,128)S(1)}, u32[]{:S(2)}, u32[]{:S(2)}) %collective-permute-start.13) | collective-permute-done | bytes 98336 | tf_op jit(solution)/shard_map/ppermute | solution.py:15
  66.6 2.6 %collective-permute-done.14 = bf16[16,512]{1,0:T(8,128)(2,1)S(1)} collective-permute-done((bf16[16,512]{1,0:T(8,128)(2,1)S(1)}, bf16[16,512]{1,0:T(8,128)(2,1)S(1)}, u32[]{:S(2)}, u32[]{:S(2)}) %collective-permute-start.14) | collective-permute-done | bytes 16416 | tf_op jit(solution)/shard_map/ppermute | solution.py:21
  69.5 13.9 %all-gather = bf16[8,32,16]{1,2,0:T(8,128)(2,1)S(1)} all-gather(bf16[1,32,16]{1,2,0:T(8,128)(2,1)S(1)} %fusion.7), channel_id=1, replica_groups=mesh['gy'=4,'gx'=8] {'gx'}, dimensions={0}, use_global_device_ids=true | all-gather | bytes 9216 | tf_op jit(solution)/shard_map/all_gather | solution.py:82
  83.5 5.6 %all_gather.7 = bf16[16,1024]{1,0:T(8,128)(2,1)S(1)} all-gather(bf16[16,256]{1,0:T(8,128)(2,1)S(1)} %bitcast.314), channel_id=1, replica_groups=mesh['gy'=4,'gx'=8] {'gy'}, dimensions={1}, use_global_device_ids=true | all-gather | bytes 40960 | tf_op jit(solution)/shard_map/all_gather | solution.py:84
  90.1 1.3 fusion.14
  91.4 1.9 %collective-permute-done.15 = bf16[16,512]{1,0:T(8,128)(2,1)S(1)} collective-permute-done((bf16[16,512]{1,0:T(8,128)(2,1)S(1)}, bf16[16,512]{1,0:T(8,128)(2,1)S(1)}, u32[]{:S(2)}, u32[]{:S(2)}) %collective-permute-start.15) | collective-permute-done | bytes 16416 | tf_op jit(solution)/shard_map/ppermute | solution.py:21
  93.3 2.7 %collective-permute-start.16 = (bf16[1,1,16,512]{3,2,1,0:T(8,128)(2,1)S(1)}, bf16[1,1,16,512]{3,2,1,0:T(8,128)(2,1)S(1)}, u32[]{:S(2)}, u32[]{:S(2)}) collective-permute-start(bf16[1,1,16,512]{3,2,1,0:T(8,128)(2,1)S(1)} %fusion.98), channel_id=1, source_target_pairs={{0,8},{8,16},{16,24},{1,9},{9,17},{17,25},{2,10},{10,18},{18,26},{... | collective-permute-start | bytes 49160 | tf_op jit(solution)/shard_map/ppermute | solution.py:12
  96.1 1.3 collective-permute-start.17
  97.4 3.2 %collective-permute-done.17 = bf16[1,1,16,512]{3,2,1,0:T(8,128)(2,1)S(1)} collective-permute-done((bf16[1,1,16,512]{3,2,1,0:T(8,128)(2,1)S(1)}, bf16[1,1,16,512]{3,2,1,0:T(8,128)(2,1)S(1)}, u32[]{:S(2)}, u32[]{:S(2)}) %collective-permute-start.17) | collective-permute-done | bytes 16416 | tf_op jit(solution)/shard_map/ppermute | solution.py:15
  100.6 6.4 %collective-permute-start.18 = (bf16[3,1,16,512]{3,2,1,0:T(8,128)(2,1)S(1)}, bf16[3,1,16,512]{3,2,1,0:T(8,128)(2,1)S(1)}, u32[]{:S(2)}, u32[]{:S(2)}) collective-permute-start(bf16[3,1,16,512]{3,2,1,0:T(8,128)(2,1)S(1)} %pad_maximum_fusion.2), channel_id=1, source_target_pairs={{0,1},{1,2},{2,3},{3,4},{4,5},{5,6},{6,7},{8,9},{9,10},{10,11},{11... | collective-permute-start | bytes 147464 | tf_op jit(solution)/shard_map/ppermute | solution.py:12
  107.0 1.9 %collective-permute-start.19 = (bf16[3,1,16,512]{3,2,1,0:T(8,128)(2,1)S(1)}, bf16[3,1,16,512]{3,2,1,0:T(8,128)(2,1)S(1)}, u32[]{:S(2)}, u32[]{:S(2)}) collective-permute-start(bf16[3,1,16,512]{3,2,1,0:T(8,128)(2,1)S(1)} %pad_maximum_fusion.2), channel_id=1, source_target_pairs={{1,0},{2,1},{3,2},{4,3},{5,4},{6,5},{7,6},{9,8},{10,9},{11,10},{12... | collective-permute-start | bytes 147464 | tf_op jit(solution)/shard_map/ppermute | solution.py:15
  109.0 3.4 %collective-permute-done.19 = bf16[3,1,16,512]{3,2,1,0:T(8,128)(2,1)S(1)} collective-permute-done((bf16[3,1,16,512]{3,2,1,0:T(8,128)(2,1)S(1)}, bf16[3,1,16,512]{3,2,1,0:T(8,128)(2,1)S(1)}, u32[]{:S(2)}, u32[]{:S(2)}) %collective-permute-start.19) | collective-permute-done | bytes 49184 | tf_op jit(solution)/shard_map/ppermute | solution.py:15
  113.5 1.8 %collective-permute-done.20 = bf16[16,512]{1,0:T(8,128)(2,1)S(1)} collective-permute-done((bf16[16,512]{1,0:T(8,128)(2,1)S(1)}, bf16[16,512]{1,0:T(8,128)(2,1)S(1)}, u32[]{:S(2)}, u32[]{:S(2)}) %collective-permute-start.20) | collective-permute-done | bytes 16416 | tf_op jit(solution)/shard_map/ppermute | solution.py:21
  115.5 4.0 %collective-permute-start.21 = (bf16[1,1,16,512]{3,2,1,0:T(8,128)(2,1)S(1)}, bf16[1,1,16,512]{3,2,1,0:T(8,128)(2,1)S(1)}, u32[]{:S(2)}, u32[]{:S(2)}) collective-permute-start(bf16[1,1,16,512]{3,2,1,0:T(8,128)(2,1)S(1)} %convert_bitcast_fusion.10), channel_id=1, source_target_pairs={{0,8},{8,16},{16,24},{1,9},{9,17},{17,25},{2,10},{10,18},{18,26},{... | collective-permute-start | bytes 49160 | tf_op jit(solution)/shard_map/ppermute | solution.py:12
  119.5 1.3 collective-permute-start.22
  120.8 3.2 %collective-permute-done.22 = bf16[1,1,16,512]{3,2,1,0:T(8,128)(2,1)S(1)} collective-permute-done((bf16[1,1,16,512]{3,2,1,0:T(8,128)(2,1)S(1)}, bf16[1,1,16,512]{3,2,1,0:T(8,128)(2,1)S(1)}, u32[]{:S(2)}, u32[]{:S(2)}) %collective-permute-start.22) | collective-permute-done | bytes 16416 | tf_op jit(solution)/shard_map/ppermute | solution.py:15
  124.0 4.5 %collective-permute-start.23 = (bf16[3,1,16,512]{3,2,1,0:T(8,128)(2,1)S(1)}, bf16[3,1,16,512]{3,2,1,0:T(8,128)(2,1)S(1)}, u32[]{:S(2)}, u32[]{:S(2)}) collective-permute-start(bf16[3,1,16,512]{3,2,1,0:T(8,128)(2,1)S(1)} %pad_maximum_fusion.3), channel_id=1, source_target_pairs={{0,1},{1,2},{2,3},{3,4},{4,5},{5,6},{6,7},{8,9},{9,10},{10,11},{11... | collective-permute-start | bytes 147464 | tf_op jit(solution)/shard_map/ppermute | solution.py:12
  128.5 1.9 %collective-permute-start.24 = (bf16[3,1,16,512]{3,2,1,0:T(8,128)(2,1)S(1)}, bf16[3,1,16,512]{3,2,1,0:T(8,128)(2,1)S(1)}, u32[]{:S(2)}, u32[]{:S(2)}) collective-permute-start(bf16[3,1,16,512]{3,2,1,0:T(8,128)(2,1)S(1)} %pad_maximum_fusion.3), channel_id=1, source_target_pairs={{1,0},{2,1},{3,2},{4,3},{5,4},{6,5},{7,6},{9,8},{10,9},{11,10},{12... | collective-permute-start | bytes 147464 | tf_op jit(solution)/shard_map/ppermute | solution.py:15
  130.4 3.5 %collective-permute-done.24 = bf16[3,1,16,512]{3,2,1,0:T(8,128)(2,1)S(1)} collective-permute-done((bf16[3,1,16,512]{3,2,1,0:T(8,128)(2,1)S(1)}, bf16[3,1,16,512]{3,2,1,0:T(8,128)(2,1)S(1)}, u32[]{:S(2)}, u32[]{:S(2)}) %collective-permute-start.24) | collective-permute-done | bytes 49184 | tf_op jit(solution)/shard_map/ppermute | solution.py:15
  134.2 1.2 collective-permute-done.25
  135.6 2.6 %collective-permute-start.26 = (bf16[1,1,16,512]{3,2,1,0:T(8,128)(2,1)S(1)}, bf16[1,1,16,512]{3,2,1,0:T(8,128)(2,1)S(1)}, u32[]{:S(2)}, u32[]{:S(2)}) collective-permute-start(bf16[1,1,16,512]{3,2,1,0:T(8,128)(2,1)S(1)} %convert_bitcast_fusion.9), channel_id=1, source_target_pairs={{0,8},{8,16},{16,24},{1,9},{9,17},{17,25},{2,10},{10,18},{18,26},{... | collective-permute-start | bytes 49160 | tf_op jit(solution)/shard_map/ppermute | solution.py:12
  138.2 1.3 collective-permute-start.27
  139.5 3.2 %collective-permute-done.27 = bf16[1,1,16,512]{3,2,1,0:T(8,128)(2,1)S(1)} collective-permute-done((bf16[1,1,16,512]{3,2,1,0:T(8,128)(2,1)S(1)}, bf16[1,1,16,512]{3,2,1,0:T(8,128)(2,1)S(1)}, u32[]{:S(2)}, u32[]{:S(2)}) %collective-permute-start.27) | collective-permute-done | bytes 16416 | tf_op jit(solution)/shard_map/ppermute | solution.py:15
  142.7 4.2 %collective-permute-start.28 = (bf16[3,1,16,512]{3,2,1,0:T(8,128)(2,1)S(1)}, bf16[3,1,16,512]{3,2,1,0:T(8,128)(2,1)S(1)}, u32[]{:S(2)}, u32[]{:S(2)}) collective-permute-start(bf16[3,1,16,512]{3,2,1,0:T(8,128)(2,1)S(1)} %pad_maximum_fusion.4), channel_id=1, source_target_pairs={{0,1},{1,2},{2,3},{3,4},{4,5},{5,6},{6,7},{8,9},{9,10},{10,11},{11... | collective-permute-start | bytes 147464 | tf_op jit(solution)/shard_map/ppermute | solution.py:12
  146.9 1.9 %collective-permute-start.29 = (bf16[3,1,16,512]{3,2,1,0:T(8,128)(2,1)S(1)}, bf16[3,1,16,512]{3,2,1,0:T(8,128)(2,1)S(1)}, u32[]{:S(2)}, u32[]{:S(2)}) collective-permute-start(bf16[3,1,16,512]{3,2,1,0:T(8,128)(2,1)S(1)} %pad_maximum_fusion.4), channel_id=1, source_target_pairs={{1,0},{2,1},{3,2},{4,3},{5,4},{6,5},{7,6},{9,8},{10,9},{11,10},{12... | collective-permute-start | bytes 147464 | tf_op jit(solution)/shard_map/ppermute | solution.py:15
  148.8 3.5 %collective-permute-done.29 = bf16[3,1,16,512]{3,2,1,0:T(8,128)(2,1)S(1)} collective-permute-done((bf16[3,1,16,512]{3,2,1,0:T(8,128)(2,1)S(1)}, bf16[3,1,16,512]{3,2,1,0:T(8,128)(2,1)S(1)}, u32[]{:S(2)}, u32[]{:S(2)}) %collective-permute-start.29) | collective-permute-done | bytes 49184 | tf_op jit(solution)/shard_map/ppermute | solution.py:15
  (97 shorter events, 8.4 us)
Async XLA Ops:
  0.0 1.3 copy-start
  0.0 2.7 %copy-start.10 = (s32[1,8,64]{2,1,0:T(8,128)S(1)}, s32[1,8,64]{2,1,0:T(8,128)}, u32[]{:S(2)}) copy-start(s32[1,8,64]{2,1,0:T(8,128)} %param.14) | copy-start | bytes 6148
  0.0 18.9 %copy-start.8 = (f32[1,3,4,512]{3,2,1,0:T(4,128)S(1)}, f32[1,3,4,512]{3,2,1,0:T(4,128)}, u32[]{:S(2)}) copy-start(f32[1,3,4,512]{3,2,1,0:T(4,128)} %param.15) | copy-start | bytes 73732
  1.5 23.2 %copy-start.1 = (bf16[1,3,512,512]{3,2,1,0:T(8,128)(2,1)S(1)}, bf16[1,3,512,512]{3,2,1,0:T(8,128)(2,1)}, u32[]{:S(2)}) copy-start(bf16[1,3,512,512]{3,2,1,0:T(8,128)(2,1)} %param.18) | copy-start | bytes 4718596
  3.1 5.2 %collective-permute-start = (f32[1,1,16,512]{3,2,1,0:T(8,128)S(1)}, f32[1,1,16,512]{3,2,1,0:T(8,128)S(1)}, u32[]{:S(2)}, u32[]{:S(2)}) collective-permute-start(f32[1,1,16,512]{3,2,1,0:T(8,128)S(1)} %broadcast_in_dim_reshape.3), channel_id=1, source_target_pairs={{0,8},{8,16},{16,24},{1,9},{9,17},{17,25},{2,10},{10,18},{18,26},{... | collective-permute-start | bytes 98312 | tf_op jit(solution)/shard_map/ppermute | solution.py:12
  7.1 4.7 %collective-permute-start.1 = (f32[1,1,16,512]{3,2,1,0:T(8,128)S(1)}, f32[1,1,16,512]{3,2,1,0:T(8,128)S(1)}, u32[]{:S(2)}, u32[]{:S(2)}) collective-permute-start(f32[1,1,16,512]{3,2,1,0:T(8,128)S(1)} %broadcast_in_dim_reshape.3), channel_id=1, source_target_pairs={{8,0},{16,8},{24,16},{9,1},{17,9},{25,17},{10,2},{18,10},{26,18},{... | collective-permute-start | bytes 98312 | tf_op jit(solution)/shard_map/ppermute | solution.py:15
  11.7 7.7 %collective-permute-start.2 = (f32[3,1,16,512]{3,2,1,0:T(8,128)S(1)}, f32[3,1,16,512]{3,2,1,0:T(8,128)S(1)}, u32[]{:S(2)}, u32[]{:S(2)}) collective-permute-start(f32[3,1,16,512]{3,2,1,0:T(8,128)S(1)} %constant_dynamic-update-slice_fusion), channel_id=1, source_target_pairs={{0,1},{1,2},{2,3},{3,4},{4,5},{5,6},{6,7},{8,9},{9,10},{10,11},{11... | collective-permute-start | bytes 294920 | tf_op jit(solution)/shard_map/ppermute | solution.py:12
  16.9 5.9 %collective-permute-start.3 = (f32[3,1,16,512]{3,2,1,0:T(8,128)S(1)}, f32[3,1,16,512]{3,2,1,0:T(8,128)S(1)}, u32[]{:S(2)}, u32[]{:S(2)}) collective-permute-start(f32[3,1,16,512]{3,2,1,0:T(8,128)S(1)} %constant_dynamic-update-slice_fusion), channel_id=1, source_target_pairs={{1,0},{2,1},{3,2},{4,3},{5,4},{6,5},{7,6},{9,8},{10,9},{11,10},{12... | collective-permute-start | bytes 294920 | tf_op jit(solution)/shard_map/ppermute | solution.py:15
  22.9 1.8 %collective-permute-start.4 = (bf16[16,512]{1,0:T(8,128)(2,1)S(1)}, bf16[16,512]{1,0:T(8,128)(2,1)S(1)}, u32[]{:S(2)}, u32[]{:S(2)}) collective-permute-start(bf16[16,512]{1,0:T(8,128)(2,1)S(1)} %fusion.94), channel_id=1, source_target_pairs={{0,1},{1,0},{2,3},{3,2},{4,5},{5,4},{6,7},{7,6},{8,9},{9,8},{10,11... | collective-permute-start | bytes 49160 | tf_op jit(solution)/shard_map/ppermute | solution.py:21
  23.3 22.7 %copy-start.2 = (bf16[1,3,512,512]{3,2,1,0:T(8,128)(2,1)S(1)}, bf16[1,3,512,512]{3,2,1,0:T(8,128)(2,1)}, u32[]{:S(2)}) copy-start(bf16[1,3,512,512]{3,2,1,0:T(8,128)(2,1)} %param.17) | copy-start | bytes 4718596
  24.9 44.5 %copy-start.6 = (bf16[1,32,512]{2,1,0:T(8,128)(2,1)S(1)}, bf16[1,32,512]{2,1,0:T(8,128)(2,1)}, u32[]{:S(2)}) copy-start(bf16[1,32,512]{2,1,0:T(8,128)(2,1)} %param.20) | copy-start | bytes 98308
  24.9 5.5 %collective-permute-start.5 = (f32[1,1,16,512]{3,2,1,0:T(8,128)S(1)}, f32[1,1,16,512]{3,2,1,0:T(8,128)S(1)}, u32[]{:S(2)}, u32[]{:S(2)}) collective-permute-start(f32[1,1,16,512]{3,2,1,0:T(8,128)S(1)} %bitcast.308), channel_id=1, source_target_pairs={{0,8},{8,16},{16,24},{1,9},{9,17},{17,25},{2,10},{10,18},{18,26},{... | collective-permute-start | bytes 98312 | tf_op jit(solution)/shard_map/ppermute | solution.py:12
  29.0 4.7 %collective-permute-start.6 = (f32[1,1,16,512]{3,2,1,0:T(8,128)S(1)}, f32[1,1,16,512]{3,2,1,0:T(8,128)S(1)}, u32[]{:S(2)}, u32[]{:S(2)}) collective-permute-start(f32[1,1,16,512]{3,2,1,0:T(8,128)S(1)} %bitcast.309), channel_id=1, source_target_pairs={{8,0},{16,8},{24,16},{9,1},{17,9},{25,17},{10,2},{18,10},{26,18},{... | collective-permute-start | bytes 98312 | tf_op jit(solution)/shard_map/ppermute | solution.py:15
  33.7 6.9 %collective-permute-start.7 = (f32[3,1,16,512]{3,2,1,0:T(8,128)S(1)}, f32[3,1,16,512]{3,2,1,0:T(8,128)S(1)}, u32[]{:S(2)}, u32[]{:S(2)}) collective-permute-start(f32[3,1,16,512]{3,2,1,0:T(8,128)S(1)} %pad_maximum_fusion), channel_id=1, source_target_pairs={{0,1},{1,2},{2,3},{3,4},{4,5},{5,6},{6,7},{8,9},{9,10},{10,11},{11... | collective-permute-start | bytes 294920 | tf_op jit(solution)/shard_map/ppermute | solution.py:12
  38.7 5.9 %collective-permute-start.8 = (f32[3,1,16,512]{3,2,1,0:T(8,128)S(1)}, f32[3,1,16,512]{3,2,1,0:T(8,128)S(1)}, u32[]{:S(2)}, u32[]{:S(2)}) collective-permute-start(f32[3,1,16,512]{3,2,1,0:T(8,128)S(1)} %pad_maximum_fusion), channel_id=1, source_target_pairs={{1,0},{2,1},{3,2},{4,3},{5,4},{6,5},{7,6},{9,8},{10,9},{11,10},{12... | collective-permute-start | bytes 294920 | tf_op jit(solution)/shard_map/ppermute | solution.py:15
  44.6 44.5 %copy-start.5 = (bf16[1,512,512]{2,1,0:T(8,128)(2,1)S(1)}, bf16[1,512,512]{2,1,0:T(8,128)(2,1)}, u32[]{:S(2)}) copy-start(bf16[1,512,512]{2,1,0:T(8,128)(2,1)} %param.19) | copy-start | bytes 1572868
  44.7 2.7 %collective-permute-start.9 = (bf16[16,512]{1,0:T(8,128)(2,1)S(1)}, bf16[16,512]{1,0:T(8,128)(2,1)S(1)}, u32[]{:S(2)}, u32[]{:S(2)}) collective-permute-start(bf16[16,512]{1,0:T(8,128)(2,1)S(1)} %fusion.85), channel_id=1, source_target_pairs={{0,2},{1,3},{2,0},{3,1},{4,6},{5,7},{6,4},{7,5},{8,10},{9,11},{10,... | collective-permute-start | bytes 49160 | tf_op jit(solution)/shard_map/ppermute | solution.py:21
  46.2 43.1 %copy-start.7 = (bf16[1024,32]{0,1:T(8,128)(2,1)S(1)}, bf16[1024,32]{0,1:T(8,128)(2,1)}, u32[]{:S(2)}) copy-start(bf16[1024,32]{0,1:T(8,128)(2,1)} %param.21) | copy-start | bytes 196612
  47.5 4.4 %collective-permute-start.10 = (f32[1,1,16,512]{3,2,1,0:T(8,128)S(1)}, f32[1,1,16,512]{3,2,1,0:T(8,128)S(1)}, u32[]{:S(2)}, u32[]{:S(2)}) collective-permute-start(f32[1,1,16,512]{3,2,1,0:T(8,128)S(1)} %bitcast.305), channel_id=1, source_target_pairs={{0,8},{8,16},{16,24},{1,9},{9,17},{17,25},{2,10},{10,18},{18,26},{... | collective-permute-start | bytes 98312 | tf_op jit(solution)/shard_map/ppermute | solution.py:12
  50.6 5.1 %collective-permute-start.11 = (f32[1,1,16,512]{3,2,1,0:T(8,128)S(1)}, f32[1,1,16,512]{3,2,1,0:T(8,128)S(1)}, u32[]{:S(2)}, u32[]{:S(2)}) collective-permute-start(f32[1,1,16,512]{3,2,1,0:T(8,128)S(1)} %bitcast.306), channel_id=1, source_target_pairs={{8,0},{16,8},{24,16},{9,1},{17,9},{25,17},{10,2},{18,10},{26,18},{... | collective-permute-start | bytes 98312 | tf_op jit(solution)/shard_map/ppermute | solution.py:15
  55.8 5.9 %collective-permute-start.12 = (f32[3,1,16,512]{3,2,1,0:T(8,128)S(1)}, f32[3,1,16,512]{3,2,1,0:T(8,128)S(1)}, u32[]{:S(2)}, u32[]{:S(2)}) collective-permute-start(f32[3,1,16,512]{3,2,1,0:T(8,128)S(1)} %pad_maximum_fusion.1), channel_id=1, source_target_pairs={{0,1},{1,2},{2,3},{3,4},{4,5},{5,6},{6,7},{8,9},{9,10},{10,11},{11... | collective-permute-start | bytes 294920 | tf_op jit(solution)/shard_map/ppermute | solution.py:12
  59.7 5.9 %collective-permute-start.13 = (f32[3,1,16,512]{3,2,1,0:T(8,128)S(1)}, f32[3,1,16,512]{3,2,1,0:T(8,128)S(1)}, u32[]{:S(2)}, u32[]{:S(2)}) collective-permute-start(f32[3,1,16,512]{3,2,1,0:T(8,128)S(1)} %pad_maximum_fusion.1), channel_id=1, source_target_pairs={{1,0},{2,1},{3,2},{4,3},{5,4},{6,5},{7,6},{9,8},{10,9},{11,10},{12... | collective-permute-start | bytes 294920 | tf_op jit(solution)/shard_map/ppermute | solution.py:15
  65.7 3.6 %collective-permute-start.14 = (bf16[16,512]{1,0:T(8,128)(2,1)S(1)}, bf16[16,512]{1,0:T(8,128)(2,1)S(1)}, u32[]{:S(2)}, u32[]{:S(2)}) collective-permute-start(bf16[16,512]{1,0:T(8,128)(2,1)S(1)} %fusion.79), channel_id=1, source_target_pairs={{0,4},{1,5},{2,6},{3,7},{4,0},{5,1},{6,2},{7,3},{8,12},{9,13},{10,... | collective-permute-start | bytes 49160 | tf_op jit(solution)/shard_map/ppermute | solution.py:21
  66.6 42.3 %copy-start.9 = (f32[1,3,4,512]{3,2,1,0:T(4,128)S(1)}, f32[1,3,4,512]{3,2,1,0:T(4,128)}, u32[]{:S(2)}) copy-start(f32[1,3,4,512]{3,2,1,0:T(4,128)} %param.16) | copy-start | bytes 73732
  89.6 25.7 %copy-start.3 = (bf16[1,3,512,512]{3,2,1,0:T(8,128)(2,1)S(1)}, bf16[1,3,512,512]{3,2,1,0:T(8,128)(2,1)}, u32[]{:S(2)}) copy-start(bf16[1,3,512,512]{3,2,1,0:T(8,128)(2,1)} %param.17) | copy-start | bytes 4718596
  89.8 3.5 %collective-permute-start.15 = (bf16[16,512]{1,0:T(8,128)(2,1)S(1)}, bf16[16,512]{1,0:T(8,128)(2,1)S(1)}, u32[]{:S(2)}, u32[]{:S(2)}) collective-permute-start(bf16[16,512]{1,0:T(8,128)(2,1)S(1)} %convolution_convert_fusion.4), channel_id=1, source_target_pairs={{0,4},{1,5},{2,6},{3,7},{4,0},{5,1},{6,2},{7,3},{8,12},{9,13},{10,... | collective-permute-start | bytes 49160 | tf_op jit(solution)/shard_map/ppermute | solution.py:21
  93.3 4.0 %collective-permute-start.16 = (bf16[1,1,16,512]{3,2,1,0:T(8,128)(2,1)S(1)}, bf16[1,1,16,512]{3,2,1,0:T(8,128)(2,1)S(1)}, u32[]{:S(2)}, u32[]{:S(2)}) collective-permute-start(bf16[1,1,16,512]{3,2,1,0:T(8,128)(2,1)S(1)} %fusion.98), channel_id=1, source_target_pairs={{0,8},{8,16},{16,24},{1,9},{9,17},{17,25},{2,10},{10,18},{18,26},{... | collective-permute-start | bytes 49160 | tf_op jit(solution)/shard_map/ppermute | solution.py:12
  96.1 4.5 %collective-permute-start.17 = (bf16[1,1,16,512]{3,2,1,0:T(8,128)(2,1)S(1)}, bf16[1,1,16,512]{3,2,1,0:T(8,128)(2,1)S(1)}, u32[]{:S(2)}, u32[]{:S(2)}) collective-permute-start(bf16[1,1,16,512]{3,2,1,0:T(8,128)(2,1)S(1)} %fusion.98), channel_id=1, source_target_pairs={{8,0},{16,8},{24,16},{9,1},{17,9},{25,17},{10,2},{18,10},{26,18},{... | collective-permute-start | bytes 49160 | tf_op jit(solution)/shard_map/ppermute | solution.py:15
  100.6 8.4 %collective-permute-start.18 = (bf16[3,1,16,512]{3,2,1,0:T(8,128)(2,1)S(1)}, bf16[3,1,16,512]{3,2,1,0:T(8,128)(2,1)S(1)}, u32[]{:S(2)}, u32[]{:S(2)}) collective-permute-start(bf16[3,1,16,512]{3,2,1,0:T(8,128)(2,1)S(1)} %pad_maximum_fusion.2), channel_id=1, source_target_pairs={{0,1},{1,2},{2,3},{3,4},{4,5},{5,6},{6,7},{8,9},{9,10},{10,11},{11... | collective-permute-start | bytes 147464 | tf_op jit(solution)/shard_map/ppermute | solution.py:12
  107.0 5.4 %collective-permute-start.19 = (bf16[3,1,16,512]{3,2,1,0:T(8,128)(2,1)S(1)}, bf16[3,1,16,512]{3,2,1,0:T(8,128)(2,1)S(1)}, u32[]{:S(2)}, u32[]{:S(2)}) collective-permute-start(bf16[3,1,16,512]{3,2,1,0:T(8,128)(2,1)S(1)} %pad_maximum_fusion.2), channel_id=1, source_target_pairs={{1,0},{2,1},{3,2},{4,3},{5,4},{6,5},{7,6},{9,8},{10,9},{11,10},{12... | collective-permute-start | bytes 147464 | tf_op jit(solution)/shard_map/ppermute | solution.py:15
  112.4 40.0 %copy-start.4 = (bf16[1,8,64,256]{3,2,1,0:T(8,128)(2,1)S(1)}, bf16[1,8,64,256]{3,2,1,0:T(8,128)(2,1)}, u32[]{:S(2)}) copy-start(bf16[1,8,64,256]{3,2,1,0:T(8,128)(2,1)} %param.13) | copy-start | bytes 786436
  112.7 2.6 %collective-permute-start.20 = (bf16[16,512]{1,0:T(8,128)(2,1)S(1)}, bf16[16,512]{1,0:T(8,128)(2,1)S(1)}, u32[]{:S(2)}, u32[]{:S(2)}) collective-permute-start(bf16[16,512]{1,0:T(8,128)(2,1)S(1)} %convolution_convert_fusion.3), channel_id=1, source_target_pairs={{0,2},{1,3},{2,0},{3,1},{4,6},{5,7},{6,4},{7,5},{8,10},{9,11},{10,... | collective-permute-start | bytes 49160 | tf_op jit(solution)/shard_map/ppermute | solution.py:21
  115.5 5.3 %collective-permute-start.21 = (bf16[1,1,16,512]{3,2,1,0:T(8,128)(2,1)S(1)}, bf16[1,1,16,512]{3,2,1,0:T(8,128)(2,1)S(1)}, u32[]{:S(2)}, u32[]{:S(2)}) collective-permute-start(bf16[1,1,16,512]{3,2,1,0:T(8,128)(2,1)S(1)} %convert_bitcast_fusion.10), channel_id=1, source_target_pairs={{0,8},{8,16},{16,24},{1,9},{9,17},{17,25},{2,10},{10,18},{18,26},{... | collective-permute-start | bytes 49160 | tf_op jit(solution)/shard_map/ppermute | solution.py:12
  119.5 4.5 %collective-permute-start.22 = (bf16[1,1,16,512]{3,2,1,0:T(8,128)(2,1)S(1)}, bf16[1,1,16,512]{3,2,1,0:T(8,128)(2,1)S(1)}, u32[]{:S(2)}, u32[]{:S(2)}) collective-permute-start(bf16[1,1,16,512]{3,2,1,0:T(8,128)(2,1)S(1)} %convert_bitcast_fusion.10), channel_id=1, source_target_pairs={{8,0},{16,8},{24,16},{9,1},{17,9},{25,17},{10,2},{18,10},{26,18},{... | collective-permute-start | bytes 49160 | tf_op jit(solution)/shard_map/ppermute | solution.py:15
  124.0 6.4 %collective-permute-start.23 = (bf16[3,1,16,512]{3,2,1,0:T(8,128)(2,1)S(1)}, bf16[3,1,16,512]{3,2,1,0:T(8,128)(2,1)S(1)}, u32[]{:S(2)}, u32[]{:S(2)}) collective-permute-start(bf16[3,1,16,512]{3,2,1,0:T(8,128)(2,1)S(1)} %pad_maximum_fusion.3), channel_id=1, source_target_pairs={{0,1},{1,2},{2,3},{3,4},{4,5},{5,6},{6,7},{8,9},{9,10},{10,11},{11... | collective-permute-start | bytes 147464 | tf_op jit(solution)/shard_map/ppermute | solution.py:12
  128.5 5.4 %collective-permute-start.24 = (bf16[3,1,16,512]{3,2,1,0:T(8,128)(2,1)S(1)}, bf16[3,1,16,512]{3,2,1,0:T(8,128)(2,1)S(1)}, u32[]{:S(2)}, u32[]{:S(2)}) collective-permute-start(bf16[3,1,16,512]{3,2,1,0:T(8,128)(2,1)S(1)} %pad_maximum_fusion.3), channel_id=1, source_target_pairs={{1,0},{2,1},{3,2},{4,3},{5,4},{6,5},{7,6},{9,8},{10,9},{11,10},{12... | collective-permute-start | bytes 147464 | tf_op jit(solution)/shard_map/ppermute | solution.py:15
  134.2 1.2 collective-permute-start.25
  135.6 3.9 %collective-permute-start.26 = (bf16[1,1,16,512]{3,2,1,0:T(8,128)(2,1)S(1)}, bf16[1,1,16,512]{3,2,1,0:T(8,128)(2,1)S(1)}, u32[]{:S(2)}, u32[]{:S(2)}) collective-permute-start(bf16[1,1,16,512]{3,2,1,0:T(8,128)(2,1)S(1)} %convert_bitcast_fusion.9), channel_id=1, source_target_pairs={{0,8},{8,16},{16,24},{1,9},{9,17},{17,25},{2,10},{10,18},{18,26},{... | collective-permute-start | bytes 49160 | tf_op jit(solution)/shard_map/ppermute | solution.py:12
  138.2 4.5 %collective-permute-start.27 = (bf16[1,1,16,512]{3,2,1,0:T(8,128)(2,1)S(1)}, bf16[1,1,16,512]{3,2,1,0:T(8,128)(2,1)S(1)}, u32[]{:S(2)}, u32[]{:S(2)}) collective-permute-start(bf16[1,1,16,512]{3,2,1,0:T(8,128)(2,1)S(1)} %convert_bitcast_fusion.9), channel_id=1, source_target_pairs={{8,0},{16,8},{24,16},{9,1},{17,9},{25,17},{10,2},{18,10},{26,18},{... | collective-permute-start | bytes 49160 | tf_op jit(solution)/shard_map/ppermute | solution.py:15
  142.7 6.2 %collective-permute-start.28 = (bf16[3,1,16,512]{3,2,1,0:T(8,128)(2,1)S(1)}, bf16[3,1,16,512]{3,2,1,0:T(8,128)(2,1)S(1)}, u32[]{:S(2)}, u32[]{:S(2)}) collective-permute-start(bf16[3,1,16,512]{3,2,1,0:T(8,128)(2,1)S(1)} %pad_maximum_fusion.4), channel_id=1, source_target_pairs={{0,1},{1,2},{2,3},{3,4},{4,5},{5,6},{6,7},{8,9},{9,10},{10,11},{11... | collective-permute-start | bytes 147464 | tf_op jit(solution)/shard_map/ppermute | solution.py:12
  146.9 5.4 %collective-permute-start.29 = (bf16[3,1,16,512]{3,2,1,0:T(8,128)(2,1)S(1)}, bf16[3,1,16,512]{3,2,1,0:T(8,128)(2,1)S(1)}, u32[]{:S(2)}, u32[]{:S(2)}) collective-permute-start(bf16[3,1,16,512]{3,2,1,0:T(8,128)(2,1)S(1)} %pad_maximum_fusion.4), channel_id=1, source_target_pairs={{1,0},{2,1},{3,2},{4,3},{5,4},{6,5},{7,6},{9,8},{10,9},{11,10},{12... | collective-permute-start | bytes 147464 | tf_op jit(solution)/shard_map/ppermute | solution.py:15
where the time goes:
time: 155 us; the launch traced here: 154 us
  starting transfers between devices  72.3 us (47%)
  waiting for transfers between devices  50.4 us (33%)
  blocking collectives  19.5 us (13%)
  matrix products  7.67 us (5%)
  local copies, waits for them, and re-layouts  3.22 us (2%)
    ppermute x12, starting transfers between devices, extended(): lax.ppermute(lax.slice_in_dim(block, block.shape[dim] - width, None, axis...  49.7 us
    ppermute x12, waiting for transfers between devices, extended(): lax.ppermute(lax.slice_in_dim(block, 0, width, axis=dim), axis, backward)  41.8 us
    ppermute x12, starting transfers between devices, extended(): lax.ppermute(lax.slice_in_dim(block, 0, width, axis=dim), axis, backward)  19.3 us
    all_gather x1, blocking collectives, body(): row_values = lax.all_gather(small, 'gx', axis=1, tiled=True)  13.9 us
    ppermute x6, waiting for transfers between devices, partner_2(): lax.ppermute(shard, axis, [(i, i ^ 1 << stride) for i in range(lax.axis_s...  8.64 us
    all_gather x1, blocking collectives, body(): lax.all_gather(row_values, 'gy', axis=1, tiled=True)  5.6 us
    ppermute x6, starting transfers between devices, partner_2(): lax.ppermute(shard, axis, [(i, i ^ 1 << stride) for i in range(lax.axis_s...  3.34 us
  transfers between devices with their start and end apart: 30, of which 17 were waited for; matrix products, arithmetic and copies ran while one was open for 3% of the time, Pallas kernels for 0%

commit v1 on v0

v1 whole, which is shorter than its diff:
```python
import functools

import jax
import jax.numpy as jnp
from jax import lax
from jax.experimental import pallas as pl
from jax.experimental.pallas import tpu as pltpu
from jax.sharding import PartitionSpec as P

MESH = pl.DeviceIdType.MESH
BF = jnp.bfloat16
F32 = jnp.float32
SELF = 9
SELF_A = 10


def dot(a, b):
    return jnp.dot(a, b, preferred_element_type=F32)


def dot_t(a, b):
    return lax.dot_general(a, b, (((1,), (1,)), ((), ())), preferred_element_type=F32)


def up_plan(level, p, q, ny, nx):
    m = 1 << level
    s = q ^ m
    odd = (q & 1) == 1
    even = (q & 1) == 0
    sends = {
        0: (p < ny - 1, p + 1, q),
        1: (p > 0, p - 1, q),
        2: (q < nx - 1, p, q + 1),
        3: (q > 0, p, q - 1),
        4: (None, p, s),
        5: (p < ny - 1, p + 1, s),
        6: (p > 0, p - 1, s),
        7: (q < nx - 1, p, (q + 1) ^ m),
        8: (q > 0, p, (q - 1) ^ m),
    }
    takes = {
        0: p > 0,
        1: p < ny - 1,
        2: q > 0,
        3: q < nx - 1,
        4: None,
        5: p > 0,
        6: p < ny - 1,
        7: s > 0,
        8: s < nx - 1,
    }
    empty = {
        0: p == 0,
        1: p == ny - 1,
        2: q == 0,
        3: q == nx - 1,
        5: p == 0,
        6: p == ny - 1,
        7: s == 0,
        8: s == nx - 1,
    }
    where = {k: k for k in range(9)}

    def also(k, send_too, take_too):
        sends[k] = (jnp.logical_and(sends[k][0], send_too),) + sends[k][1:]
        takes[k] = jnp.logical_and(takes[k], take_too)

    if level == 0:
        also(2, odd, even)
        also(3, even, odd)
        also(7, odd, odd)
        also(8, even, even)
        where[2] = jnp.where(even, 2, 4)
        where[3] = jnp.where(even, 4, 3)
        where[7] = jnp.where(even, SELF, 7)
        where[8] = jnp.where(even, 8, SELF)
    elif level == 1:
        high = (q & m) != 0
        low = (q & m) == 0
        also(7, (((q + 1) ^ m) & m) != 0, high)
        also(8, (((q - 1) ^ m) & m) == 0, low)
        where[7] = jnp.where(low, 3, 7)
        where[8] = jnp.where(low, 8, 2)
    return sends, takes, empty, where


def down_plan(level, p, q, ny, nx):
    m = 1 << level
    s = q ^ m
    odd = (q & 1) == 1
    even = (q & 1) == 0
    sends = {
        4: (None, p, s),
        5: (p < ny - 1, p + 1, s),
        6: (p > 0, p - 1, s),
        7: (s < nx - 1, p, s + 1),
        8: (s > 0, p, s - 1),
        0: (p < ny - 1, p + 1, q),
        1: (p > 0, p - 1, q),
        2: (q < nx - 1, p, q + 1),
        3: (q > 0, p, q - 1),
    }
    takes = {
        4: None,
        0: p > 0,
        1: p < ny - 1,
        2: q > 0,
        3: q < nx - 1,
        5: p > 0,
        6: p < ny - 1,
        7: q > 0,
        8: q < nx - 1,
    }
    empty = {
        0: p == 0,
        1: p == ny - 1,
        2: q == 0,
        3: q == nx - 1,
        5: p == 0,
        6: p == ny - 1,
        7: q == 0,
        8: q == nx - 1,
    }
    where = {k: k for k in range(9)}
    if level == 0:
        sends[7] = (jnp.logical_and(sends[7][0], even),) + sends[7][1:]
        sends[8] = (jnp.logical_and(sends[8][0], odd),) + sends[8][1:]
        takes[7] = jnp.logical_and(takes[7], even)
        takes[8] = jnp.logical_and(takes[8], odd)
        where[7] = jnp.where(even, 7, SELF)
        where[8] = jnp.where(even, SELF, 8)
    return sends, takes, empty, where


def when(cond, run):
    if cond is None:
        run()
    else:
        pl.when(cond)(run)


def kernel(
    ny,
    nx,
    pack,
    fields,
    leaf_inverse,
    coupling,
    index,
    up_coef,
    down_coef,
    merge_own,
    merge_other,
    top_inverse,
    compress,
    couple,
    out,
    f_v,
    inv_v,
    coup_v,
    idx_v,
    upc_v,
    dnc_v,
    own_v,
    other_v,
    top_v,
    comp_v,
    wide_v,
    tc_v,
    sib_v,
    zbuf,
    abuf,
    c1,
    call,
    solved_v,
    d_v,
    lsem,
    up_send,
    up_recv,
    co_send,
    co_recv,
    dn_send,
    dn_recv,
    g1_send,
    g1_recv,
    g2_send,
    g2_recv,
):
    boxes, size, _ = inv_v.shape
    skel = coup_v.shape[1]
    levels = own_v.shape[0]
    kt = comp_v.shape[0]
    groups = call.shape[0]
    per_row = nx // pack
    p = lax.axis_index("gy")
    q = lax.axis_index("gx")
    me = p * nx + q
    count = ny * nx

    local = []

    def fetch(src, dst):
        copy = pltpu.make_async_copy(src, dst, lsem.at[len(local)])
        copy.start()
        local.append(copy)
        return copy

    get_f = fetch(fields.at[0], f_v)
    get_idx = fetch(index.at[0], idx_v)
    half = boxes // 2
    get_inv = [
        fetch(leaf_inverse.at[0, pl.ds(i * half, half)], inv_v.at[pl.ds(i * half, half)])
        for i in range(2)
    ]
    get_coup = fetch(coupling.at[0], coup_v)
    get_upc = fetch(up_coef.at[0], upc_v)
    get_merge = [
        (fetch(merge_own.at[0, l], own_v.at[l]), fetch(merge_other.at[0, l], other_v.at[l]))
        for l in range(levels)
    ]
    place = lax.rem(q, pack)
    wide_v[...] = jnp.zeros_like(wide_v)
    get_wide = fetch(compress.at[0], wide_v.at[pl.ds(pl.multiple_of(place * kt, kt), kt)])
    get_comp = fetch(compress.at[0], comp_v)
    get_top = fetch(top_inverse.at[0], top_v)
    get_tc = fetch(couple, tc_v)
    get_dnc = fetch(down_coef.at[0], dnc_v)

    ups = [up_plan(l, p, q, ny, nx) for l in range(levels)]
    downs = [down_plan(l, p, q, ny, nx) for l in range(levels)]

    def clear(buf, l, k):
        def run():
            buf[l, k] = jnp.zeros(buf.shape[2:], buf.dtype)

        return run

    for l in range(levels):
        for k, cond in ups[l][2].items():
            pl.when(cond)(clear(zbuf, l, k))
        for k, cond in downs[l][2].items():
            pl.when(cond)(clear(abuf, l, k))

    barrier = pltpu.get_barrier_semaphore()

    def greet(j, carry):
        t = lax.rem(me + j, count)
        pl.semaphore_signal(
            barrier, inc=1, device_id=(t // nx, lax.rem(t, nx)), device_id_type=MESH
        )
        return carry

    lax.fori_loop(1, count, greet, 0)

    get_f.wait()
    get_idx.wait()
    rows = lax.broadcasted_iota(jnp.int32, (size, skel), 0)

    def selector(k):
        return jnp.where(rows == idx_v[k : k + 1, :], 1.0, 0.0).astype(BF)

    state = []
    for k in range(boxes):
        if k % half == 0:
            get_inv[k // half].wait()
        if k == 0:
            get_coup.wait()
        b = f_v[:, k * size : (k + 1) * size]
        solved = dot(b, inv_v[k]).astype(BF)
        solved_v[:, k * size : (k + 1) * size] = solved
        state.append(dot(b, selector(k)) - dot_t(solved, coup_v[k]))
    state = jnp.concatenate(state, axis=1)

    def fold(k):
        eye = (
            lax.broadcasted_iota(jnp.int32, (skel, skel), 0)
            == lax.broadcasted_iota(jnp.int32, (skel, skel), 1)
        )
        chosen = dot_t(jnp.where(eye, 1.0, 0.0).astype(BF), selector(k))
        d_v[k] = (chosen - dot(coup_v[k], inv_v[k])).astype(BF)

    def copy_of(buf, l, source, k, target, send, recv):
        return pltpu.make_async_remote_copy(
            src_ref=buf.at[l, source],
            dst_ref=buf.at[l, k],
            send_sem=send.at[l, k],
            recv_sem=recv.at[l, k],
            device_id=target,
            device_id_type=MESH,
        )

    def start(buf, l, source, plan, k, send, recv):
        cond, tp, tq = plan[0][k]
        when(cond, lambda: copy_of(buf, l, source, k, (tp, tq), send, recv).start())

    def arrive(buf, l, source, plan, k, send, recv):
        cond = plan[1][k]
        when(cond, lambda: copy_of(buf, l, source, k, (p, q), send, recv).wait_recv())

    def sent(buf, l, source, plan, k, send, recv):
        cond = plan[0][k][0]
        when(cond, lambda: copy_of(buf, l, source, k, (p, q), send, recv).wait_send())

    def coef_copy(l):
        return pltpu.make_async_remote_copy(
            src_ref=upc_v.at[l],
            dst_ref=sib_v.at[l],
            send_sem=co_send.at[l],
            recv_sem=co_recv.at[l],
            device_id=(p, q ^ (1 << l)),
            device_id_type=MESH,
        )

    def mix(values, coefs, parts):
        total = coefs[0:1] * parts[0] + coefs[1:2] * parts[1]
        return values - (total + coefs[2:3] * parts[2] + coefs[3:4] * parts[3])

    get_upc.wait()
    pl.semaphore_wait(barrier, count - 1)
    folds = list(range(boxes))
    each = -(-boxes // levels)

    for l in range(levels):
        plan = ups[l]
        where = plan[3]
        zbuf[l, SELF] = state.astype(BF)
        if l == 0:
            coef_copy(0).start()
        for k in (4, 5, 6, 7, 8, 0, 1, 2, 3):
            start(zbuf, l, SELF, plan, k, up_send, up_recv)
        if l == 0:
            for other_level in range(1, levels):
                coef_copy(other_level).start()
        for k in folds[l * each : (l + 1) * each]:
            fold(k)
        if l > 0:
            for k in range(9):
                sent(zbuf, l - 1, SELF, ups[l - 1], k, up_send, up_recv)
        get_merge[l][0].wait()
        get_merge[l][1].wait()
        first = (0, 1, 2, 3, 4) if l == 0 else (0, 1, 2, 3)
        for k in first:
            arrive(zbuf, l, SELF, plan, k, up_send, up_recv)
        g = mix(state, upc_v[l], [zbuf[l, where[k]].astype(F32) for k in range(4)]).astype(BF)
        total = dot(g, own_v[l])
        for k in range(len(first), 9):
            arrive(zbuf, l, SELF, plan, k, up_send, up_recv)
        coef_copy(l).wait_recv()
        g = mix(
            zbuf[l, 4].astype(F32),
            sib_v[l],
            [zbuf[l, where[k]].astype(F32) for k in range(5, 9)],
        ).astype(BF)
        state = total + dot(g, other_v[l])

    top = state.astype(BF)
    get_wide.wait()
    small = dot_t(top, wide_v[...]).astype(BF)
    c1[pack - 1] = small

    def first_copy(j):
        return pltpu.make_async_remote_copy(
            src_ref=c1.at[pack - 1],
            dst_ref=c1.at[j - 1],
            send_sem=g1_send.at[j - 1],
            recv_sem=g1_recv.at[j - 1],
            device_id=(p, q ^ j),
            device_id_type=MESH,
        )

    for j in range(1, pack):
        first_copy(j).start()
    get_top.wait()
    state = dot(top, top_v[...])
    for j in range(1, pack):
        first_copy(j).wait_recv()
    joined = small.astype(F32)
    for j in range(1, pack):
        joined = joined + c1[j - 1].astype(F32)
    group = p * per_row + q // pack
    call[group] = joined.astype(BF)

    def second_copy(j):
        t = lax.rem(group + j, groups)
        return pltpu.make_async_remote_copy(
            src_ref=call.at[group],
            dst_ref=call.at[group],
            send_sem=g2_send.at[t],
            recv_sem=g2_recv.at[group],
            device_id=(t // per_row, lax.rem(t, per_row) * pack + place),
            device_id_type=MESH,
        )

    def second_from(j):
        t = lax.rem(group + j, groups)
        return pltpu.make_async_remote_copy(
            src_ref=call.at[t],
            dst_ref=call.at[t],
            send_sem=g2_send.at[t],
            recv_sem=g2_recv.at[t],
            device_id=(p, q),
            device_id_type=MESH,
        )

    def over_groups(run):
        if groups <= 8:
            for j in range(1, groups):
                run(j)
        else:
            def step(j, carry):
                run(j)
                return carry

            lax.fori_loop(1, groups, step, 0)

    over_groups(lambda j: second_copy(j).start())
    for j in range(1, pack):
        first_copy(j).wait_send()
    for k in range(9):
        sent(zbuf, levels - 1, SELF, ups[levels - 1], k, up_send, up_recv)
    for l in range(levels):
        coef_copy(l).wait_send()
    get_tc.wait()
    get_comp.wait()
    get_dnc.wait()
    over_groups(lambda j: second_from(j).wait_recv())
    if groups <= 8:
        coarse = dot_t(jnp.concatenate([call[g] for g in range(groups)], axis=1), tc_v[...])
    else:
        width = call.shape[2]

        def add(g, total):
            columns = pl.ds(pl.multiple_of(g * width, width), width)
            return total + dot_t(call[g], tc_v[:, columns])

        coarse = lax.fori_loop(0, groups, add, jnp.zeros((call.shape[1], kt), F32))
    state = state + dot(coarse.astype(BF), comp_v[...])

    for l in reversed(range(levels)):
        plan = downs[l]
        where = plan[3]
        r = state.astype(BF)
        abuf[l, SELF] = dot_t(r, other_v[l]).astype(BF)
        for k in (4, 5, 6, 7, 8):
            start(abuf, l, SELF, plan, k, dn_send, dn_recv)
        mine = dot_t(r, own_v[l])
        abuf[l, SELF_A] = mine.astype(BF)
        for k in (0, 1, 2, 3):
            start(abuf, l, SELF_A, plan, k, dn_send, dn_recv)
        if l == levels - 1:
            over_groups(lambda j: second_copy(j).wait_send())
        else:
            for k in range(9):
                source = SELF_A if k < 4 else SELF
                sent(abuf, l + 1, source, downs[l + 1], k, dn_send, dn_recv)
        for k in (4, 5, 6, 7, 8, 0, 1, 2, 3):
            arrive(abuf, l, SELF, plan, k, dn_send, dn_recv)
        parts = [
            abuf[l, where[d]].astype(F32) + abuf[l, where[5 + d]].astype(F32) for d in range(4)
        ]
        state = mix(mine + abuf[l, 4].astype(F32), dnc_v[l], parts)

    w = state.astype(BF)
    for k in range(boxes):
        part = dot(w[:, k * skel : (k + 1) * skel], d_v[k])
        columns = slice(k * size, (k + 1) * size)
        out[0, :, columns] = solved_v[:, columns].astype(F32) + part
    for k in range(9):
        source = SELF_A if k < 4 else SELF
        sent(abuf, 0, source, downs[0], k, dn_send, dn_recv)


def body(ny, nx, *args):
    (fields, leaf_inverse, coupling, index, up_coef, down_coef, merge_own, merge_other) = args[:8]
    top_inverse, compress, top_couple = args[8:]
    count = fields.shape[1]
    points = fields.shape[2]
    boxes, size = leaf_inverse.shape[1:3]
    skel = coupling.shape[2]
    levels, total = merge_own.shape[1:3]
    kt = compress.shape[1]
    pack = 128 // kt
    groups = ny * nx // pack
    couple = top_couple.T
    dma = pltpu.SemaphoreType.DMA
    scratch = [
        pltpu.VMEM((count, points), BF),
        pltpu.VMEM((boxes, size, size), BF),
        pltpu.VMEM((boxes, skel, size), BF),
        pltpu.VMEM((boxes, skel), jnp.int32),
        pltpu.VMEM((levels, 4, total), F32),
        pltpu.VMEM((levels, 4, total), F32),
        pltpu.VMEM((levels, total, total), BF),
        pltpu.VMEM((levels, total, total), BF),
        pltpu.VMEM((total, total), BF),
        pltpu.VMEM((kt, total), BF),
        pltpu.VMEM((pack * kt, total), BF),
        pltpu.VMEM(couple.shape, BF),
        pltpu.VMEM((levels, 4, total), F32),
        pltpu.VMEM((levels, 10, count, total), BF),
        pltpu.VMEM((levels, 11, count, total), BF),
        pltpu.VMEM((pack, count, pack * kt), BF),
        pltpu.VMEM((groups, count, pack * kt), BF),
        pltpu.VMEM((count, points), BF),
        pltpu.VMEM((boxes, skel, size), BF),
        dma((11 + 2 * levels,)),
        dma((levels, 9)),
        dma((levels, 9)),
        dma((levels,)),
        dma((levels,)),
        dma((levels, 9)),
        dma((levels, 9)),
        dma((pack,)),
        dma((pack,)),
        dma((groups,)),
        dma((groups,)),
    ]
    return pl.pallas_call(
        functools.partial(kernel, ny, nx, pack),
        out_shape=jax.ShapeDtypeStruct(fields.shape, F32),
        in_specs=[pl.BlockSpec(memory_space=pl.ANY)] * 11,
        out_specs=pl.BlockSpec(memory_space=pltpu.VMEM),
        scratch_shapes=scratch,
        compiler_params=pltpu.CompilerParams(
            collective_id=0, has_side_effects=True, vmem_limit_bytes=40 * 1024 * 1024
        ),
    )(
        fields, leaf_inverse, coupling, index, up_coef, down_coef, merge_own, merge_other,
        top_inverse, compress, couple,
    )


def solution(mesh):
    placed = (
        P("gy", None, "gx"),
        P("gy", "gx", None, None),
        P("gy", "gx", None, None),
        P("gy", "gx", None),
        P("gy", "gx", None, None),
        P("gy", "gx", None, None),
        P("gy", "gx", None, None),
        P("gy", "gx", None, None),
        P("gy", "gx", None),
        P("gy", "gx", None),
        P(None, ("gy", "gx")),
    )
    return jax.shard_map(
        functools.partial(body, mesh.shape["gy"], mesh.shape["gx"]),
        mesh=mesh,
        in_specs=placed,
        out_specs=P("gy", None, "gx"),
        check_vma=False,
    )
```

time: 155 us -> 54 us (0.35)
  the two profiles are of different devices: /device:TPU:1 before, /device:TPU:0 now
where the time goes in v1:
time: 54 us; the launch traced here: 53.4 us
  Pallas kernels  42.1 us (78%)
  local copies, waits for them, and re-layouts  11.3 us (21%)
    pallas_call x1, Pallas kernels, body(): pl.pallas_call(functools.partial(kernel, ny, nx, pack), out_shape=jax.Sha...  42.1 us
    unnamed x23, local copies, waits for them, and re-layouts  11.3 us

profile of v1, /device:TPU:0, one launch (start us, length us, event | category | flops | bytes accessed | tf_op | source)
XLA Modules:
  0.0 53.4 jit_solution(9556302559638122285)
XLA Ops:
  0.0 0.0 copy-start
  0.0 1.4 %copy-done = bf16[1,3,512,512]{3,2,1,0:T(8,128)(2,1)S(1)} copy-done((bf16[1,3,512,512]{3,2,1,0:T(8,128)(2,1)S(1)}, bf16[1,3,512,512]{3,2,1,0:T(8,128)(2,1)}, u32[]{:S(2)}) %copy-start) | copy-done | bytes 1572888
  1.4 0.0 copy-start.1
  1.4 1.4 %copy-done.1 = bf16[1,3,512,512]{3,2,1,0:T(8,128)(2,1)S(1)} copy-done((bf16[1,3,512,512]{3,2,1,0:T(8,128)(2,1)S(1)}, bf16[1,3,512,512]{3,2,1,0:T(8,128)(2,1)}, u32[]{:S(2)}) %copy-start.1) | copy-done | bytes 1572888
  2.8 0.0 copy-start.2
  2.8 1.2 %copy-done.2 = bf16[1,8,256,256]{3,2,1,0:T(8,128)(2,1)S(1)} copy-done((bf16[1,8,256,256]{3,2,1,0:T(8,128)(2,1)S(1)}, bf16[1,8,256,256]{3,2,1,0:T(8,128)(2,1)}, u32[]{:S(2)}) %copy-start.2) | copy-done | bytes 1048600
  4.0 0.0 copy-start.3
  4.0 1.0 %copy-done.3 = bf16[1,512,512]{2,1,0:T(8,128)(2,1)S(1)} copy-done((bf16[1,512,512]{2,1,0:T(8,128)(2,1)S(1)}, bf16[1,512,512]{2,1,0:T(8,128)(2,1)}, u32[]{:S(2)}) %copy-start.3) | copy-done | bytes 524312
  5.1 0.0 copy-start.4
  5.1 0.9 %copy-done.4 = bf16[1,8,64,256]{3,2,1,0:T(8,128)(2,1)S(1)} copy-done((bf16[1,8,64,256]{3,2,1,0:T(8,128)(2,1)S(1)}, bf16[1,8,64,256]{3,2,1,0:T(8,128)(2,1)}, u32[]{:S(2)}) %copy-start.4) | copy-done | bytes 262168
  6.0 0.0 copy-start.5
  6.0 0.8 %copy-done.5 = bf16[1,16,2048]{2,1,0:T(8,128)(2,1)S(1)} copy-done((bf16[1,16,2048]{2,1,0:T(8,128)(2,1)S(1)}, bf16[1,16,2048]{2,1,0:T(8,128)(2,1)}, u32[]{:S(2)}) %copy-start.5) | copy-done | bytes 65560
  6.9 0.0 copy-start.6
  6.9 0.8 %copy-done.6 = bf16[1024,32]{0,1:T(8,128)(2,1)S(1)} copy-done((bf16[1024,32]{0,1:T(8,128)(2,1)S(1)}, bf16[1024,32]{0,1:T(8,128)(2,1)}, u32[]{:S(2)}) %copy-start.6) | copy-done | bytes 65560
  7.7 0.0 copy-start.7
  7.7 0.8 %copy-done.7 = bf16[1,32,512]{2,1,0:T(8,128)(2,1)S(1)} copy-done((bf16[1,32,512]{2,1,0:T(8,128)(2,1)S(1)}, bf16[1,32,512]{2,1,0:T(8,128)(2,1)}, u32[]{:S(2)}) %copy-start.7) | copy-done | bytes 32792
  8.5 0.0 copy-start.8
  8.5 0.7 %copy-done.8 = f32[1,3,4,512]{3,2,1,0:T(4,128)S(1)} copy-done((f32[1,3,4,512]{3,2,1,0:T(4,128)S(1)}, f32[1,3,4,512]{3,2,1,0:T(4,128)}, u32[]{:S(2)}) %copy-start.8) | copy-done | bytes 24600
  9.2 0.0 copy-start.9
  9.2 0.7 %copy-done.9 = f32[1,3,4,512]{3,2,1,0:T(4,128)S(1)} copy-done((f32[1,3,4,512]{3,2,1,0:T(4,128)S(1)}, f32[1,3,4,512]{3,2,1,0:T(4,128)}, u32[]{:S(2)}) %copy-start.9) | copy-done | bytes 24600
  9.9 0.0 copy-start.10
  10.0 0.7 %copy-done.10 = s32[1,8,64]{2,1,0:T(8,128)S(1)} copy-done((s32[1,8,64]{2,1,0:T(8,128)S(1)}, s32[1,8,64]{2,1,0:T(8,128)}, u32[]{:S(2)}) %copy-start.10) | copy-done | bytes 2072
  10.6 42.1 %shard_map.109 = f32[1,16,2048]{2,1,0:T(8,128)S(1)} custom-call(bf16[1,16,2048]{2,1,0:T(8,128)(2,1)S(1)} %copy-done.5, bf16[1,8,256,256]{3,2,1,0:T(8,128)(2,1)S(1)} %copy-done.2, bf16[1,8,64,256]{3,2,1,0:T(8,128)(2,1)S(1)} %copy-done.4, s32[1,8,64]{2,1,0:T(8,128)S(1)} %copy-done.10, f32[1,3,4,512]{3,2,1,0:T(4,128)S(1)} %copy-done.8, ...), custom_call_target="tpu_custom_call" | custom-call | tf_op jit(solution)/shard_map/pallas_call | solution.py:518
  52.7 0.7 %copy.13 = f32[1,16,2048]{2,1,0:T(8,128)} copy(f32[1,16,2048]{2,1,0:T(8,128)S(1)} %shard_map.109) | data formatting | bytes 262144
Async XLA Ops:
  0.0 1.4 %copy-start = (bf16[1,3,512,512]{3,2,1,0:T(8,128)(2,1)S(1)}, bf16[1,3,512,512]{3,2,1,0:T(8,128)(2,1)}, u32[]{:S(2)}) copy-start(bf16[1,3,512,512]{3,2,1,0:T(8,128)(2,1)} %merge_own.1) | copy-start | bytes 4718596
  1.4 1.4 %copy-start.1 = (bf16[1,3,512,512]{3,2,1,0:T(8,128)(2,1)S(1)}, bf16[1,3,512,512]{3,2,1,0:T(8,128)(2,1)}, u32[]{:S(2)}) copy-start(bf16[1,3,512,512]{3,2,1,0:T(8,128)(2,1)} %merge_other.1) | copy-start | bytes 4718596
  2.8 1.2 %copy-start.2 = (bf16[1,8,256,256]{3,2,1,0:T(8,128)(2,1)S(1)}, bf16[1,8,256,256]{3,2,1,0:T(8,128)(2,1)}, u32[]{:S(2)}) copy-start(bf16[1,8,256,256]{3,2,1,0:T(8,128)(2,1)} %leaf_inverse.1) | copy-start | bytes 3145732
  4.0 1.0 %copy-start.3 = (bf16[1,512,512]{2,1,0:T(8,128)(2,1)S(1)}, bf16[1,512,512]{2,1,0:T(8,128)(2,1)}, u32[]{:S(2)}) copy-start(bf16[1,512,512]{2,1,0:T(8,128)(2,1)} %top_inverse.1) | copy-start | bytes 1572868
  5.1 0.9 %copy-start.4 = (bf16[1,8,64,256]{3,2,1,0:T(8,128)(2,1)S(1)}, bf16[1,8,64,256]{3,2,1,0:T(8,128)(2,1)}, u32[]{:S(2)}) copy-start(bf16[1,8,64,256]{3,2,1,0:T(8,128)(2,1)} %coupling.1) | copy-start | bytes 786436
  6.0 0.8 %copy-start.5 = (bf16[1,16,2048]{2,1,0:T(8,128)(2,1)S(1)}, bf16[1,16,2048]{2,1,0:T(8,128)(2,1)}, u32[]{:S(2)}) copy-start(bf16[1,16,2048]{2,1,0:T(8,128)(2,1)} %fields.1) | copy-start | bytes 196612
  6.9 0.8 %copy-start.6 = (bf16[1024,32]{0,1:T(8,128)(2,1)S(1)}, bf16[1024,32]{0,1:T(8,128)(2,1)}, u32[]{:S(2)}) copy-start(bf16[1024,32]{0,1:T(8,128)(2,1)} %param.21) | copy-start | bytes 196612
  7.7 0.8 %copy-start.7 = (bf16[1,32,512]{2,1,0:T(8,128)(2,1)S(1)}, bf16[1,32,512]{2,1,0:T(8,128)(2,1)}, u32[]{:S(2)}) copy-start(bf16[1,32,512]{2,1,0:T(8,128)(2,1)} %compress.1) | copy-start | bytes 98308
  8.5 0.7 %copy-start.8 = (f32[1,3,4,512]{3,2,1,0:T(4,128)S(1)}, f32[1,3,4,512]{3,2,1,0:T(4,128)}, u32[]{:S(2)}) copy-start(f32[1,3,4,512]{3,2,1,0:T(4,128)} %up_coef.1) | copy-start | bytes 73732
  9.2 0.7 %copy-start.9 = (f32[1,3,4,512]{3,2,1,0:T(4,128)S(1)}, f32[1,3,4,512]{3,2,1,0:T(4,128)}, u32[]{:S(2)}) copy-start(f32[1,3,4,512]{3,2,1,0:T(4,128)} %down_coef.1) | copy-start | bytes 73732
  9.9 0.7 %copy-start.10 = (s32[1,8,64]{2,1,0:T(8,128)S(1)}, s32[1,8,64]{2,1,0:T(8,128)}, u32[]{:S(2)}) copy-start(s32[1,8,64]{2,1,0:T(8,128)} %index.1) | copy-start | bytes 6148

commit v2 on v1

--- a/solution.py
+++ b/solution.py
@@ -243,14 +243,34 @@
 
     barrier = pltpu.get_barrier_semaphore()
 
-    def greet(j, carry):
-        t = lax.rem(me + j, count)
-        pl.semaphore_signal(
-            barrier, inc=1, device_id=(t // nx, lax.rem(t, nx)), device_id_type=MESH
-        )
-        return carry
-
-    lax.fori_loop(1, count, greet, 0)
+    def greet(tp, tq):
+        pl.semaphore_signal(barrier, inc=1, device_id=(tp, tq), device_id_type=MESH)
+
+    if nx == 8 and ny == 4 and pack == 4:
+        met = nx - 1
+        for turn in range(1, nx):
+            greet(p, q ^ turn)
+        for turn in range(1, ny):
+            tp = p ^ turn
+            beside = jnp.logical_or(tp == p + 1, tp == p - 1)
+            for flip in (0, 4):
+                greet(tp, q ^ flip)
+
+            @pl.when(beside)
+            def _():
+                for flip in (1, 2):
+                    greet(tp, q ^ flip)
+
+            met = met + jnp.where(beside, 4, 2)
+    else:
+        met = count - 1
+
+        def greet_one(j, carry):
+            t = lax.rem(me + j, count)
+            greet(t // nx, lax.rem(t, nx))
+            return carry
+
+        lax.fori_loop(1, count, greet_one, 0)
 
     get_f.wait()
     get_idx.wait()
@@ -316,7 +336,7 @@
         return values - (total + coefs[2:3] * parts[2] + coefs[3:4] * parts[3])
 
     get_upc.wait()
-    pl.semaphore_wait(barrier, count - 1)
+    pl.semaphore_wait(barrier, met)
     folds = list(range(boxes))
     each = -(-boxes // levels)
 
@@ -518,11 +538,11 @@
     return pl.pallas_call(
         functools.partial(kernel, ny, nx, pack),
         out_shape=jax.ShapeDtypeStruct(fields.shape, F32),
-        in_specs=[pl.BlockSpec(memory_space=pl.ANY)] * 11,
+        in_specs=[pl.BlockSpec(memory_space=pltpu.HBM)] * 11,
         out_specs=pl.BlockSpec(memory_space=pltpu.VMEM),
         scratch_shapes=scratch,
         compiler_params=pltpu.CompilerParams(
-            collective_id=0, has_side_effects=True, vmem_limit_bytes=40 * 1024 * 1024
+            collective_id=0, has_side_effects=True, vmem_limit_bytes=62 * 1024 * 1024
         ),
     )(
         fields, leaf_inverse, coupling, index, up_coef, down_coef, merge_own, merge_other,

time: 54 us -> 43.3 us (0.80)
  local copies, waits for them, and re-layouts: 11.3 us -> 1.57 us
  Pallas kernels: 42.1 us -> 41.5 us
    unnamed x23 -> x1, local copies, waits for them, and re-layouts: 11.3 us -> 1.57 us
    pallas_call x1, Pallas kernels: 42.1 us -> 41.5 us  [body(): pl.pallas_call(functools.partial(kernel, ny, nx, pack), out_shape=jax.Sha...]
where the time goes in v2:
time: 43.3 us; the launch traced here: 43.1 us
  Pallas kernels  41.5 us (96%)
  local copies, waits for them, and re-layouts  1.57 us (4%)
    pallas_call x1, Pallas kernels, body(): pl.pallas_call(functools.partial(kernel, ny, nx, pack), out_shape=jax.Sha...  41.5 us
    unnamed x1, local copies, waits for them, and re-layouts  1.57 us

profile of v2, /device:TPU:0, one launch (start us, length us, event | category | flops | bytes accessed | tf_op | source)
XLA Modules:
  0.0 43.1 jit_solution(11166730431493392845)
XLA Ops:
  0.0 41.5 %shard_map.109 = f32[1,16,2048]{2,1,0:T(8,128)} custom-call(bf16[1,16,2048]{2,1,0:T(8,128)(2,1)} %fields.1, bf16[1,8,256,256]{3,2,1,0:T(8,128)(2,1)} %leaf_inverse.1, bf16[1,8,64,256]{3,2,1,0:T(8,128)(2,1)} %coupling.1, s32[1,8,64]{2,1,0:T(8,128)} %index.1, f32[1,3,4,512]{3,2,1,0:T(4,128)} %up_coef.1, f32[1,3,4,512]{3,2,1,0:T(4,128)} %down_coef.1, ...), custom_call_target="tpu_custom_call" | custom-call | tf_op jit(solution)/shard_map/pallas_call | solution.py:538
  41.5 1.6 %copy.13 = f32[1,16,2048]{2,1,0:T(8,128)} copy(f32[1,16,2048]{2,1,0:T(8,128)} %shard_map.109) | data formatting | bytes 262144
